TPU v7x, 512 devices: a whole 4x8x8 slice. The times are simulated.
512 devices in a mesh: sta: 8 (over x, core), tm: 32 (over y, z_hi), tpl: 2 (over z_lo).
Axes of the slice: x: 4, y: 8, z: 8 (z_hi: 4, z_lo: 2; z = z_hi * 2 + z_lo), core: 2. Of those that a mesh axis runs over, the one named last changes fastest.
Arguments:
- waveforms: bfloat16 [8, 32768], P('sta', 'tm'), may hold values from -120 to 120
- templates: bfloat16 [512, 300], P('tpl'), may hold values from -0.375 to 0.375
- moveouts: int32 [8, 512], P('sta', 'tpl'), may hold values from 0 to 719
- channel_mask: int32 [8, 512], P('sta', 'tpl'), may hold values 0 or 1
Outputs:
- stack: bfloat16 [512, 32768], P('tpl', 'tm')
All inputs are finite; a program needn't handle non-finite values. No bound on the sum of `channel_mask` on one device may be relied on, other than what follows from the above.
Results may differ from a plain program's by a relative error of at most 0.015.
Values may be sent and summed in bfloat16 or wider, within the bound.
No kernel may reach another device: no remote copies, remote signals or barrier semaphores. Data moves between devices by JAX's collectives and lax.ppermute only.
A program may use at most 64 MiB of HBM per device.

v0:
```python
import functools
import math

import jax
import jax.numpy as jnp
from jax import lax
from jax.experimental import pallas as pl
from jax.experimental.pallas import tpu as pltpu
from jax.sharding import PartitionSpec as P

MOVE = 720
EPSILON = 1e-05
LANES = 128
ROW_STEP = 17


def rolled_left(x, by):
    return x if by == 0 else pltpu.roll(x, x.shape[1] - by, 1)


def pack_kernel(wave_ref, moves_ref, mask_ref, out_ref):
    moves = moves_ref[...]
    fields = (wave_ref[...].astype(jnp.float32), moves >> 7, moves & 127, mask_ref[...])
    line = jnp.concatenate([field.astype(jnp.float32) for field in fields], axis=1)
    half = line.shape[1] // 2
    lines = jnp.concatenate([line[:, :half], line[:, half:]], axis=0).astype(jnp.bfloat16)
    out_ref[...] = jnp.broadcast_to(lines[None], out_ref.shape)


def stack_kernel(
    base_ref, turn_ref, here_ref, next_ref, bank_ref, out_ref, rms_ref, rows_ref, toeplitz, normed, total,
    *, template_len, stations, block_len, bank,
):
    depth = toeplitz.shape[0]
    blocks = toeplitz.shape[1] // LANES
    out_blocks = block_len // LANES
    station_rows = bank * ROW_STEP
    half = here_ref.shape[2]
    samples = jnp.concatenate(
        [
            here_ref[:, 0, :].astype(jnp.float32),
            here_ref[:, 1, : block_len - half].astype(jnp.float32),
            next_ref[:, 0, :].astype(jnp.float32),
            next_ref[:, 1, : block_len - half].astype(jnp.float32),
            jnp.zeros((stations, LANES), jnp.float32),
        ],
        axis=1,
    )
    width = samples.shape[1]

    window = samples * samples
    energy, covered, size = None, 0, 1
    while covered < template_len:
        if template_len & size:
            moved = rolled_left(window, covered)
            energy = moved if energy is None else energy + moved
            covered = covered + size
        window = window + rolled_left(window, size)
        size = 2 * size
    rms_ref[...] = lax.rsqrt(energy / template_len + EPSILON) * (1.0 / math.sqrt(stations))

    for step in range(8):
        moved = rolled_left(samples, step)
        for block in range(width // LANES):
            row = (block * 8 + step) * stations
            rows_ref[row : row + stations, :] = moved[:, block * LANES : (block + 1) * LANES]
    normed[stations * station_rows : stations * station_rows + 16, :] = jnp.zeros((16, LANES), jnp.float32)

    @pl.loop(0, stations)
    def _(s):
        eight = jnp.concatenate(
            [rows_ref[pl.ds(block * 8 * stations + s, 8, stride=stations), :] for block in range(width // LANES)],
            axis=1,
        )
        for group in range(LANES // 16):
            pair = jnp.concatenate(
                [rolled_left(eight, 16 * group), rolled_left(eight, 16 * group + 8)], axis=0
            ).astype(jnp.bfloat16)
            for part in range(-(-depth // LANES)):
                row = part * LANES + 16 * group
                if row < depth:
                    toeplitz[row : row + 16, :] = pair[:, part * LANES : (part + blocks) * LANES]
        for column in range(blocks // 2):
            span = slice(2 * column * LANES, (2 * column + 2) * LANES)
            correlated = jnp.dot(bank_ref[...], toeplitz[:, span], preferred_element_type=jnp.float32)
            scaled = correlated * rms_ref[pl.ds(s, 1), span]
            for k in range(0, bank, 8):
                for half in range(2):
                    row = s * station_rows + k * ROW_STEP + 2 * column + half
                    normed[pl.ds(row, 8, stride=ROW_STEP), :] = scaled[k : k + 8, half * LANES : (half + 1) * LANES]

    lane = lax.broadcasted_iota(jnp.int32, (out_blocks, LANES), 1)

    @pl.loop(0, bank // 16)
    def _(pair):
        for one in range(16):
            k = pair * 16 + one
            summed = None
            for s in range(stations):
                base = base_ref[s * bank + k]
                turn = turn_ref[s * bank + k]
                picked = jnp.where(
                    lane >= LANES - turn, normed[pl.ds(base, out_blocks), :], normed[pl.ds(base + 1, out_blocks), :]
                )
                moved = pltpu.roll(picked, turn & (LANES - 1), 1)
                summed = moved if summed is None else summed + moved
            row = pair * 16 * out_blocks + (one // 8) * 8 * out_blocks + one % 8
            total[pl.ds(row, out_blocks, stride=8), :] = summed
    for k in range(0, bank, 16):
        for block in range(out_blocks):
            upper = total[k * out_blocks + 8 * block : k * out_blocks + 8 * block + 8, :]
            row = (k + 8) * out_blocks + 8 * block
            lower = total[row : row + 8, :]
            out_ref[k : k + 16, block * LANES : (block + 1) * LANES] = jnp.concatenate(
                [upper, lower], axis=0
            ).astype(jnp.bfloat16)


def shards(waveforms, templates, moveouts, channel_mask):
    block_len = waveforms.shape[1]
    bank, template_len = templates.shape
    stations = lax.axis_size("sta") * waveforms.shape[0]
    depth = -(-template_len // 16) * 16
    blocks = -(-(block_len + MOVE) // (2 * LANES)) * 2
    in_vmem = pl.BlockSpec(memory_space=pltpu.VMEM)
    in_smem = pl.BlockSpec(memory_space=pltpu.SMEM)

    packed = pl.pallas_call(
        pack_kernel,
        out_shape=jax.ShapeDtypeStruct((stations, 2, (block_len + 3 * bank) // 2), jnp.bfloat16),
        in_specs=[in_vmem] * 3,
        out_specs=in_vmem,
    )(waveforms, moveouts, channel_mask)
    here = lax.all_to_all(packed, "sta", 0, 0, tiled=True)
    count = lax.axis_size("tm")
    after = lax.ppermute(here, "tm", [(i, i - 1) for i in range(1, count)])

    here, templates = lax.optimization_barrier((here, templates))
    fields = here[:, 1, block_len - here.shape[2] :].astype(jnp.int32)
    coarse, fine, mask = jnp.split(fields, 3, axis=1)
    first = (jnp.arange(stations)[:, None] * bank + jnp.arange(bank)[None, :]) * ROW_STEP
    base = jnp.where(mask != 0, first + coarse, stations * bank * ROW_STEP).reshape(-1)
    turn = (LANES - fine).reshape(-1)
    bank_rows = jnp.pad(templates, ((0, 0), (0, depth - template_len)))

    return pl.pallas_call(
        functools.partial(
            stack_kernel, template_len=template_len, stations=stations, block_len=block_len, bank=bank
        ),
        out_shape=jax.ShapeDtypeStruct((bank, block_len), jnp.bfloat16),
        in_specs=[in_smem, in_smem, in_vmem, in_vmem, in_vmem],
        out_specs=in_vmem,
        scratch_shapes=[
            pltpu.VMEM((stations, 2 * block_len + LANES), jnp.float32),
            pltpu.VMEM((8 * stations * (2 * block_len // LANES + 1), LANES), jnp.float32),
            pltpu.VMEM((depth, blocks * LANES), jnp.bfloat16),
            pltpu.VMEM((stations * bank * ROW_STEP + 16, LANES), jnp.float32),
            pltpu.VMEM((bank * block_len // LANES, LANES), jnp.float32),
        ],
        compiler_params=pltpu.CompilerParams(vmem_limit_bytes=48 * 1024 * 1024),
    )(base, turn, here, after, bank_rows)


def solution(mesh):
    in_specs = (P("sta", "tm"), P("tpl", None), P("sta", "tpl"), P("sta", "tpl"))
    out_specs = P("tpl", "tm")
    return jax.shard_map(shards, mesh=mesh, in_specs=in_specs, out_specs=out_specs, check_vma=False)
```

profile of v0, /device:TPU:40, one launch (start us, length us, event | category | flops | bytes accessed | tf_op | source)
XLA Modules:
  0.0 37.1 jit_solution(2546420411598741941)
XLA Ops:
  0.0 0.0 copy-start
  0.0 1.4 %shard_map.46 = bf16[8,2,896]{2,1,0:T(2,128)(2,1)} custom-call(bf16[1,1024]{1,0:T(2,128)(2,1)} %wave_ref.1, s32[1,256]{1,0:T(1,128)} %moves_ref.1, s32[1,256]{1,0:T(1,128)} %mask_ref.1), custom_call_target="tpu_custom_call" | custom-call | tf_op jit(solution)/shard_map/pallas_call | solution.py:128
  1.4 4.3 %all-to-all-start = ((bf16[8,2,896]{2,1,0:T(2,128)(2,1)}), bf16[8,2,896]{2,1,0:T(2,128)(2,1)S(1)}, u32[]{:S(2)}, u32[]{:S(2)}) async-start(bf16[8,2,896]{2,1,0:T(2,128)(2,1)} %shard_map.46), calls=%async_computation | async-start | bytes 57344 | tf_op jit(solution)/shard_map/all_to_all | solution.py:134
  5.7 5.4 %all-to-all-done.here_ref = bf16[8,2,896]{2,1,0:T(2,128)(2,1)S(1)} async-done(((bf16[8,2,896]{2,1,0:T(2,128)(2,1)}), bf16[8,2,896]{2,1,0:T(2,128)(2,1)S(1)}, u32[]{:S(2)}, u32[]{:S(2)}) %all-to-all-start) | async-done | bytes 28704 | tf_op jit(solution)/shard_map/all_to_all | solution.py:134
  11.2 11.7 %collective-permute-start = (bf16[8,2,896]{2,1,0:T(2,128)(2,1)S(1)}, bf16[8,2,896]{2,1,0:T(2,128)(2,1)S(1)}, u32[]{:S(2)}, u32[]{:S(2)}) collective-permute-start(bf16[8,2,896]{2,1,0:T(2,128)(2,1)S(1)} %all-to-all-done.here_ref), channel_id=1, source_target_pairs={{2,0},{4,2},{6,4},{8,6},{10,8},{12,10},{14,12},{16,14},{18,16},{20... | collective-permute-start | bytes 86024 | tf_op jit(solution)/shard_map/ppermute | solution.py:136
  22.9 0.1 fusion
  23.0 0.0 copy-done
  23.0 0.2 copy.5
  23.2 1.2 %collective-permute-done.next_ref = bf16[8,2,896]{2,1,0:T(2,128)(2,1)S(1)} collective-permute-done((bf16[8,2,896]{2,1,0:T(2,128)(2,1)S(1)}, bf16[8,2,896]{2,1,0:T(2,128)(2,1)S(1)}, u32[]{:S(2)}, u32[]{:S(2)}) %collective-permute-start) | collective-permute-done | bytes 28704 | tf_op jit(solution)/shard_map/ppermute | solution.py:136
  24.4 12.7 %shard_map.47 = bf16[256,1024]{1,0:T(8,128)(2,1)} custom-call(s32[2048]{0:T(1024)S(1)} %bitcast.10, s32[2048]{0:T(1024)S(1)} %bitcast.9, bf16[8,2,896]{2,1,0:T(2,128)(2,1)S(1)} %all-to-all-done.here_ref, bf16[8,2,896]{2,1,0:T(2,128)(2,1)S(1)} %collective-permute-done.next_ref, bf16[256,304]{1,0:T(8,128)(2,1)S(1)} %pad.4.bank_ref), custom_call_target="tpu_custom_call" | custom-call | tf_op jit(solution)/shard_map/pallas_call | solution.py:146
  (6 shorter events, 0.1 us)
Async XLA Ops:
  0.0 23.0 %copy-start = (bf16[256,300]{0,1:T(8,128)(2,1)S(1)}, bf16[256,300]{0,1:T(8,128)(2,1)}, u32[]{:S(2)}) copy-start(bf16[256,300]{0,1:T(8,128)(2,1)} %param.5) | copy-start | bytes 460804
  1.4 9.7 %all-to-all-start = ((bf16[8,2,896]{2,1,0:T(2,128)(2,1)}), bf16[8,2,896]{2,1,0:T(2,128)(2,1)S(1)}, u32[]{:S(2)}, u32[]{:S(2)}) async-start(bf16[8,2,896]{2,1,0:T(2,128)(2,1)} %shard_map.46), calls=%async_computation | async-start | bytes 57344 | tf_op jit(solution)/shard_map/all_to_all | solution.py:134
  11.2 13.3 %collective-permute-start = (bf16[8,2,896]{2,1,0:T(2,128)(2,1)S(1)}, bf16[8,2,896]{2,1,0:T(2,128)(2,1)S(1)}, u32[]{:S(2)}, u32[]{:S(2)}) collective-permute-start(bf16[8,2,896]{2,1,0:T(2,128)(2,1)S(1)} %all-to-all-done.here_ref), channel_id=1, source_target_pairs={{2,0},{4,2},{6,4},{8,6},{10,8},{12,10},{14,12},{16,14},{18,16},{20... | collective-permute-start | bytes 86024 | tf_op jit(solution)/shard_map/ppermute | solution.py:136
where the time goes:
time: 37.3 us; the launch traced here: 37.1 us
  starting transfers between devices  16 us (43%)
  Pallas kernels  14 us (38%)
  waiting for transfers between devices  6.66 us (18%)
    pallas_call x1, Pallas kernels, shards(): pl.pallas_call(functools.partial(stack_kernel, template_len=template_len,...  12.7 us
    ppermute x1, starting transfers between devices, shards(): after = lax.ppermute(here, 'tm', [(i, i - 1) for i in range(1, count)])  11.7 us
    all_to_all x1, waiting for transfers between devices, shards(): here = lax.all_to_all(packed, 'sta', 0, 0, tiled=True)  5.42 us
    all_to_all x1, starting transfers between devices, shards(): here = lax.all_to_all(packed, 'sta', 0, 0, tiled=True)  4.3 us
    pallas_call x1, Pallas kernels, shards(): pl.pallas_call(pack_kernel, out_shape=jax.ShapeDtypeStruct((stations, 2,...  1.37 us
    ppermute x1, waiting for transfers between devices, shards(): after = lax.ppermute(here, 'tm', [(i, i - 1) for i in range(1, count)])  1.24 us
  transfers between devices with their start and end apart: 2, of which 2 were waited for; matrix products, arithmetic and copies ran while one was open for 1% of the time, Pallas kernels for 0%

commit v1 on v0

--- a/solution.py
+++ b/solution.py
@@ -28,13 +28,13 @@
 
 
 def stack_kernel(
-    base_ref, turn_ref, here_ref, next_ref, bank_ref, out_ref, rms_ref, rows_ref, toeplitz, normed, total,
+    base_ref, turn_ref, here_ref, next_ref, bank_ref, out_ref,
+    rms_ref, rows_ref, toeplitz_even, toeplitz_odd, normed_even, normed_odd, total,
     *, template_len, stations, block_len, bank,
 ):
-    depth = toeplitz.shape[0]
-    blocks = toeplitz.shape[1] // LANES
+    depth = toeplitz_even.shape[0]
+    blocks = toeplitz_even.shape[1] // LANES
     out_blocks = block_len // LANES
-    station_rows = bank * ROW_STEP
     half = here_ref.shape[2]
     samples = jnp.concatenate(
         [
@@ -64,10 +64,12 @@
         for block in range(width // LANES):
             row = (block * 8 + step) * stations
             rows_ref[row : row + stations, :] = moved[:, block * LANES : (block + 1) * LANES]
-    normed[stations * station_rows : stations * station_rows + 16, :] = jnp.zeros((16, LANES), jnp.float32)
+    for normed in (normed_even, normed_odd):
+        normed[bank * ROW_STEP : bank * ROW_STEP + 16, :] = jnp.zeros((16, LANES), jnp.float32)
+    total[...] = jnp.zeros_like(total)
+    lane = lax.broadcasted_iota(jnp.int32, (out_blocks, LANES), 1)
 
-    @pl.loop(0, stations)
-    def _(s):
+    def lay_out(s, toeplitz):
         eight = jnp.concatenate(
             [rows_ref[pl.ds(block * 8 * stations + s, 8, stride=stations), :] for block in range(width // LANES)],
             axis=1,
@@ -80,40 +82,46 @@
                 row = part * LANES + 16 * group
                 if row < depth:
                     toeplitz[row : row + 16, :] = pair[:, part * LANES : (part + blocks) * LANES]
-        for column in range(blocks // 2):
-            span = slice(2 * column * LANES, (2 * column + 2) * LANES)
-            correlated = jnp.dot(bank_ref[...], toeplitz[:, span], preferred_element_type=jnp.float32)
-            scaled = correlated * rms_ref[pl.ds(s, 1), span]
-            for k in range(0, bank, 8):
-                for half in range(2):
-                    row = s * station_rows + k * ROW_STEP + 2 * column + half
-                    normed[pl.ds(row, 8, stride=ROW_STEP), :] = scaled[k : k + 8, half * LANES : (half + 1) * LANES]
 
-    lane = lax.broadcasted_iota(jnp.int32, (out_blocks, LANES), 1)
+    def correlate(s, toeplitz, normed, column):
+        span = slice(2 * column * LANES, (2 * column + 2) * LANES)
+        correlated = jnp.dot(bank_ref[...], toeplitz[:, span], preferred_element_type=jnp.float32)
+        scaled = correlated * rms_ref[pl.ds(s, 1), span]
+        for k in range(0, bank, 8):
+            for one in range(2):
+                row = k * ROW_STEP + 2 * column + one
+                normed[pl.ds(row, 8, stride=ROW_STEP), :] = scaled[k : k + 8, one * LANES : (one + 1) * LANES]
 
-    @pl.loop(0, bank // 16)
+    def add_moved(entry, normed, templates):
+        for k in templates:
+            base = base_ref[entry * bank + k]
+            turn = turn_ref[entry * bank + k]
+            picked = jnp.where(
+                lane >= LANES - turn, normed[pl.ds(base, out_blocks), :], normed[pl.ds(base + 1, out_blocks), :]
+            )
+            rows = slice(k * out_blocks, (k + 1) * out_blocks)
+            total[rows, :] = total[rows, :] + pltpu.roll(picked, turn & (LANES - 1), 1)
+
+    def stage(s, toeplitz, normed, previous):
+        columns = blocks // 2
+        for column in range(columns):
+            correlate(s, toeplitz, normed, column)
+            add_moved(s, previous, range(bank * column // columns, bank * (column + 1) // columns))
+
+    @pl.loop(0, stations // 2)
     def _(pair):
-        for one in range(16):
-            k = pair * 16 + one
-            summed = None
-            for s in range(stations):
-                base = base_ref[s * bank + k]
-                turn = turn_ref[s * bank + k]
-                picked = jnp.where(
-                    lane >= LANES - turn, normed[pl.ds(base, out_blocks), :], normed[pl.ds(base + 1, out_blocks), :]
-                )
-                moved = pltpu.roll(picked, turn & (LANES - 1), 1)
-                summed = moved if summed is None else summed + moved
-            row = pair * 16 * out_blocks + (one // 8) * 8 * out_blocks + one % 8
-            total[pl.ds(row, out_blocks, stride=8), :] = summed
+        lay_out(2 * pair, toeplitz_even)
+        stage(2 * pair, toeplitz_even, normed_even, normed_odd)
+        lay_out(2 * pair + 1, toeplitz_odd)
+        stage(2 * pair + 1, toeplitz_odd, normed_odd, normed_even)
+
+    add_moved(stations, normed_odd, range(bank))
     for k in range(0, bank, 16):
         for block in range(out_blocks):
-            upper = total[k * out_blocks + 8 * block : k * out_blocks + 8 * block + 8, :]
-            row = (k + 8) * out_blocks + 8 * block
-            lower = total[row : row + 8, :]
-            out_ref[k : k + 16, block * LANES : (block + 1) * LANES] = jnp.concatenate(
-                [upper, lower], axis=0
-            ).astype(jnp.bfloat16)
+            halves = [total[pl.ds(part * out_blocks + block, 8, stride=out_blocks), :] for part in (k, k + 8)]
+            out_ref[k : k + 16, block * LANES : (block + 1) * LANES] = jnp.concatenate(halves, axis=0).astype(
+                jnp.bfloat16
+            )
 
 
 def shards(waveforms, templates, moveouts, channel_mask):
@@ -138,9 +146,10 @@
     here, templates = lax.optimization_barrier((here, templates))
     fields = here[:, 1, block_len - here.shape[2] :].astype(jnp.int32)
     coarse, fine, mask = jnp.split(fields, 3, axis=1)
-    first = (jnp.arange(stations)[:, None] * bank + jnp.arange(bank)[None, :]) * ROW_STEP
-    base = jnp.where(mask != 0, first + coarse, stations * bank * ROW_STEP).reshape(-1)
-    turn = (LANES - fine).reshape(-1)
+    first = jnp.arange(bank)[None, :] * ROW_STEP
+    base = jnp.where(mask != 0, first + coarse, bank * ROW_STEP)
+    base = jnp.pad(base, ((1, 0), (0, 0)), constant_values=bank * ROW_STEP).reshape(-1)
+    turn = jnp.pad(LANES - fine, ((1, 0), (0, 0)), constant_values=LANES).reshape(-1)
     bank_rows = jnp.pad(templates, ((0, 0), (0, depth - template_len)))
 
     return pl.pallas_call(
@@ -154,7 +163,9 @@
             pltpu.VMEM((stations, 2 * block_len + LANES), jnp.float32),
             pltpu.VMEM((8 * stations * (2 * block_len // LANES + 1), LANES), jnp.float32),
             pltpu.VMEM((depth, blocks * LANES), jnp.bfloat16),
-            pltpu.VMEM((stations * bank * ROW_STEP + 16, LANES), jnp.float32),
+            pltpu.VMEM((depth, blocks * LANES), jnp.bfloat16),
+            pltpu.VMEM((bank * ROW_STEP + 16, LANES), jnp.float32),
+            pltpu.VMEM((bank * ROW_STEP + 16, LANES), jnp.float32),
             pltpu.VMEM((bank * block_len // LANES, LANES), jnp.float32),
         ],
         compiler_params=pltpu.CompilerParams(vmem_limit_bytes=48 * 1024 * 1024),

time: 37.3 us -> 33.7 us (0.903)
  Pallas kernels: 14 us -> 10.3 us
    pallas_call x1, Pallas kernels: 12.7 us -> 8.95 us  [shards(): pl.pallas_call(functools.partial(stack_kernel, template_len=template_len,...]
where the time goes in v1:
time: 33.7 us; the launch traced here: 33.5 us
  starting transfers between devices  16.2 us (48%)
  Pallas kernels  10.3 us (31%)
  waiting for transfers between devices  6.68 us (20%)
    ppermute x1, starting transfers between devices, shards(): after = lax.ppermute(here, 'tm', [(i, i - 1) for i in range(1, count)])  11.7 us
    pallas_call x1, Pallas kernels, shards(): pl.pallas_call(functools.partial(stack_kernel, template_len=template_len,...  8.95 us
    all_to_all x1, waiting for transfers between devices, shards(): here = lax.all_to_all(packed, 'sta', 0, 0, tiled=True)  5.42 us
    all_to_all x1, starting transfers between devices, shards(): here = lax.all_to_all(packed, 'sta', 0, 0, tiled=True)  4.43 us
    pallas_call x1, Pallas kernels, shards(): pl.pallas_call(pack_kernel, out_shape=jax.ShapeDtypeStruct((stations, 2,...  1.33 us
    ppermute x1, waiting for transfers between devices, shards(): after = lax.ppermute(here, 'tm', [(i, i - 1) for i in range(1, count)])  1.26 us
  transfers between devices with their start and end apart: 2, of which 2 were waited for; matrix products, arithmetic and copies ran while one was open for 1% of the time, Pallas kernels for 0%

profile of v1, /device:TPU:40, one launch (start us, length us, event | category | flops | bytes accessed | tf_op | source)
XLA Modules:
  0.0 33.5 jit_solution(8234519290631433126)
XLA Ops:
  0.0 1.3 %shard_map.46 = bf16[8,2,896]{2,1,0:T(2,128)(2,1)} custom-call(bf16[1,1024]{1,0:T(2,128)(2,1)} %wave_ref.1, s32[1,256]{1,0:T(1,128)} %moves_ref.1, s32[1,256]{1,0:T(1,128)} %mask_ref.1), custom_call_target="tpu_custom_call" | custom-call | tf_op jit(solution)/shard_map/pallas_call | solution.py:136
  1.3 0.0 copy-start
  1.3 4.4 %all-to-all-start = ((bf16[8,2,896]{2,1,0:T(2,128)(2,1)}), bf16[8,2,896]{2,1,0:T(2,128)(2,1)S(1)}, u32[]{:S(2)}, u32[]{:S(2)}) async-start(bf16[8,2,896]{2,1,0:T(2,128)(2,1)} %shard_map.46), calls=%async_computation | async-start | bytes 57344 | tf_op jit(solution)/shard_map/all_to_all | solution.py:142
  5.8 5.4 %all-to-all-done.here_ref = bf16[8,2,896]{2,1,0:T(2,128)(2,1)S(1)} async-done(((bf16[8,2,896]{2,1,0:T(2,128)(2,1)}), bf16[8,2,896]{2,1,0:T(2,128)(2,1)S(1)}, u32[]{:S(2)}, u32[]{:S(2)}) %all-to-all-start) | async-done | bytes 28704 | tf_op jit(solution)/shard_map/all_to_all | solution.py:142
  11.3 11.7 %collective-permute-start = (bf16[8,2,896]{2,1,0:T(2,128)(2,1)S(1)}, bf16[8,2,896]{2,1,0:T(2,128)(2,1)S(1)}, u32[]{:S(2)}, u32[]{:S(2)}) collective-permute-start(bf16[8,2,896]{2,1,0:T(2,128)(2,1)S(1)} %all-to-all-done.here_ref), channel_id=1, source_target_pairs={{2,0},{4,2},{6,4},{8,6},{10,8},{12,10},{14,12},{16,14},{18,16},{20... | collective-permute-start | bytes 86024 | tf_op jit(solution)/shard_map/ppermute | solution.py:144
  23.0 0.0 copy-done
  23.1 0.2 copy.5
  23.3 1.3 %collective-permute-done.next_ref = bf16[8,2,896]{2,1,0:T(2,128)(2,1)S(1)} collective-permute-done((bf16[8,2,896]{2,1,0:T(2,128)(2,1)S(1)}, bf16[8,2,896]{2,1,0:T(2,128)(2,1)S(1)}, u32[]{:S(2)}, u32[]{:S(2)}) %collective-permute-start) | collective-permute-done | bytes 28704 | tf_op jit(solution)/shard_map/ppermute | solution.py:144
  24.5 9.0 %shard_map.47 = bf16[256,1024]{1,0:T(8,128)(2,1)} custom-call(s32[2304]{0:T(1024)S(1)} %reshape.13.base_ref, s32[2304]{0:T(1024)S(1)} %reshape.14.turn_ref, bf16[8,2,896]{2,1,0:T(2,128)(2,1)S(1)} %all-to-all-done.here_ref, bf16[8,2,896]{2,1,0:T(2,128)(2,1)S(1)} %collective-permute-done.next_ref, bf16[256,304]{1,0:T(8,128)(2,1)S(1)} %pad.13.bank_ref), custom_call_target="tpu_custom_call" | custom-call | tf_op jit(solution)/shard_map/pallas_call | solution.py:155
  (9 shorter events, 0.1 us)
Async XLA Ops:
  1.3 21.7 %copy-start = (bf16[256,300]{0,1:T(8,128)(2,1)S(1)}, bf16[256,300]{0,1:T(8,128)(2,1)}, u32[]{:S(2)}) copy-start(bf16[256,300]{0,1:T(8,128)(2,1)} %param.5) | copy-start | bytes 460804
  1.3 9.9 %all-to-all-start = ((bf16[8,2,896]{2,1,0:T(2,128)(2,1)}), bf16[8,2,896]{2,1,0:T(2,128)(2,1)S(1)}, u32[]{:S(2)}, u32[]{:S(2)}) async-start(bf16[8,2,896]{2,1,0:T(2,128)(2,1)} %shard_map.46), calls=%async_computation | async-start | bytes 57344 | tf_op jit(solution)/shard_map/all_to_all | solution.py:142
  11.3 13.3 %collective-permute-start = (bf16[8,2,896]{2,1,0:T(2,128)(2,1)S(1)}, bf16[8,2,896]{2,1,0:T(2,128)(2,1)S(1)}, u32[]{:S(2)}, u32[]{:S(2)}) collective-permute-start(bf16[8,2,896]{2,1,0:T(2,128)(2,1)S(1)} %all-to-all-done.here_ref), channel_id=1, source_target_pairs={{2,0},{4,2},{6,4},{8,6},{10,8},{12,10},{14,12},{16,14},{18,16},{20... | collective-permute-start | bytes 86024 | tf_op jit(solution)/shard_map/ppermute | solution.py:144

commit v2 on v0

v2 whole, which is shorter than its diff:
```python
import functools
import math

import jax
import jax.numpy as jnp
from jax import lax
from jax.experimental import pallas as pl
from jax.experimental.pallas import tpu as pltpu
from jax.sharding import PartitionSpec as P

MOVE = 720
EPSILON = 1e-05
LANES = 128
ROW_STEP = 17
WIDE = 14
PIECE = 64


def rolled_left(x, by):
    return x if by == 0 else pltpu.roll(x, x.shape[1] - by, 1)


def pack_kernel(wave_hbm, moves_hbm, mask_hbm, out_ref, wave_ref, moves_ref, mask_ref, sems):
    given = ((wave_hbm, wave_ref), (moves_hbm, moves_ref), (mask_hbm, mask_ref))
    copies = [pltpu.make_async_copy(source, target, sems.at[i]) for i, (source, target) in enumerate(given)]
    for copy in copies:
        copy.start()
    for copy in copies:
        copy.wait()
    moves = moves_ref[...]
    fields = (wave_ref[...].astype(jnp.float32), moves >> 7, moves & 127, mask_ref[...])
    line = jnp.concatenate([field.astype(jnp.float32) for field in fields], axis=1)
    half = line.shape[1] // 2
    lines = jnp.concatenate([line[:, :half], line[:, half:]], axis=0).astype(jnp.bfloat16)
    out_ref[...] = jnp.broadcast_to(lines[None], out_ref.shape)


def stack_kernel(
    moves_ref, here_ref, next_ref, bank_ref, out_ref,
    places, moves_sem, stacked, out_sem, rms_ref, rows_ref, toeplitz_a, toeplitz_b, toeplitz_c, toeplitz_d, normed_a, normed_b, normed_c, normed_d, total,
    *, template_len, stations, block_len, bank,
):
    depth = toeplitz_a.shape[0]
    blocks = toeplitz_a.shape[1] // LANES
    out_blocks = block_len // LANES
    half = here_ref.shape[2]
    fetch = pltpu.make_async_copy(moves_ref, places, moves_sem)
    fetch.start()
    samples = jnp.concatenate(
        [
            here_ref[:, 0, :].astype(jnp.float32),
            here_ref[:, 1, : block_len - half].astype(jnp.float32),
            next_ref[:, 0, :].astype(jnp.float32),
            next_ref[:, 1, : block_len - half].astype(jnp.float32),
            jnp.zeros((stations, LANES), jnp.float32),
        ],
        axis=1,
    )
    width = samples.shape[1]

    window = samples * samples
    energy, covered, size = None, 0, 1
    while covered < template_len:
        if template_len & size:
            moved = rolled_left(window, covered)
            energy = moved if energy is None else energy + moved
            covered = covered + size
        window = window + rolled_left(window, size)
        size = 2 * size
    rms_ref[...] = lax.rsqrt(energy / template_len + EPSILON) * (1.0 / math.sqrt(stations))

    for step in range(8):
        moved = rolled_left(samples, step)
        for block in range(width // LANES):
            row = (block * 8 + step) * stations
            rows_ref[row : row + stations, :] = moved[:, block * LANES : (block + 1) * LANES]
    for normed in (normed_a, normed_b, normed_c, normed_d):
        normed[bank * ROW_STEP : bank * ROW_STEP + 16, :] = jnp.zeros((16, LANES), jnp.float32)
    lane = lax.broadcasted_iota(jnp.int32, (out_blocks, LANES), 1)

    def lay_out(s, group, toeplitz):
        eight = jnp.concatenate(
            [rows_ref[pl.ds(block * 8 * stations + s, 8, stride=stations), :] for block in range(width // LANES)],
            axis=1,
        )
        pair = jnp.concatenate(
            [rolled_left(eight, 16 * group), rolled_left(eight, 16 * group + 8)], axis=0
        ).astype(jnp.bfloat16)
        for part in range(-(-depth // LANES)):
            row = part * LANES + 16 * group
            if row < depth:
                toeplitz[row : row + 16, :] = pair[:, part * LANES : (part + blocks) * LANES]

    def correlate(s, toeplitz, normed, first, last):
        span = slice(first * LANES, last * LANES)
        correlated = jnp.dot(bank_ref[...], toeplitz[:, span], preferred_element_type=jnp.float32)
        scaled = correlated * rms_ref[s : s + 1, span]
        for k in range(0, bank, 8):
            for block in range(first, last):
                row = k * ROW_STEP + block
                column = (block - first) * LANES
                normed[pl.ds(row, 8, stride=ROW_STEP), :] = scaled[k : k + 8, column : column + LANES]

    def add_moved(members, buffers, templates):
        for k in templates:
            rows = slice(k * out_blocks, (k + 1) * out_blocks)
            summed = None if members[0] == 0 else total[rows, :]
            for s, normed in zip(members, buffers):
                base = places[s * bank + k]
                turn = places[(stations + s) * bank + k]
                picked = jnp.where(
                    lane >= LANES - turn, normed[pl.ds(base, out_blocks), :], normed[pl.ds(base + 1, out_blocks), :]
                )
                moved = pltpu.roll(picked, turn & (LANES - 1), 1)
                summed = moved if summed is None else summed + moved
            total[rows, :] = summed

    toeplitz = ((toeplitz_a, toeplitz_b), (toeplitz_c, toeplitz_d))
    normed = ((normed_a, normed_b), (normed_c, normed_d))
    members = [(s, s + 1) for s in range(0, stations - 2, 2)] + [(stations - 2,), (stations - 1,)]
    spans = [(first, min(first + WIDE, blocks)) for first in range(0, blocks, WIDE)]
    groups = LANES // 16

    def stage(p):
        jobs = [(one, span) for span in spans for one in range(len(members[p]))]
        for j, (one, span) in enumerate(jobs):
            share = lambda amount: range(amount * j // len(jobs), amount * (j + 1) // len(jobs))
            correlate(members[p][one], toeplitz[p % 2][one], normed[p % 2][one], *span)
            if p + 1 < len(members):
                for step in share(len(members[p + 1]) * groups):
                    lay_out(members[p + 1][step // groups], step % groups, toeplitz[(p + 1) % 2][step // groups])
            if p > 0:
                add_moved(members[p - 1], normed[(p - 1) % 2], share(bank))

    for one in range(2):
        for group in range(groups):
            lay_out(members[0][one], group, toeplitz[0][one])
    fetch.wait()
    for p in range(len(members)):
        stage(p)
    writes = []
    for first in range(0, bank, PIECE):
        add_moved(members[-1], normed[(len(members) - 1) % 2], range(first, first + PIECE))
        for k in range(first, first + PIECE, 16):
            for block in range(out_blocks):
                halves = [total[pl.ds(part * out_blocks + block, 8, stride=out_blocks), :] for part in (k, k + 8)]
                stacked[k : k + 16, block * LANES : (block + 1) * LANES] = jnp.concatenate(halves, axis=0).astype(
                    jnp.bfloat16
                )
        piece = pl.ds(first, PIECE)
        writes.append(pltpu.make_async_copy(stacked.at[piece], out_ref.at[piece], out_sem.at[first // PIECE]))
        writes[-1].start()
    for write in writes:
        write.wait()


def shards(waveforms, templates, moveouts, channel_mask):
    block_len = waveforms.shape[1]
    bank, template_len = templates.shape
    stations = lax.axis_size("sta") * waveforms.shape[0]
    depth = -(-template_len // 16) * 16
    blocks = -(-(block_len + MOVE) // (2 * LANES)) * 2
    in_vmem = pl.BlockSpec(memory_space=pltpu.VMEM)

    packed = pl.pallas_call(
        pack_kernel,
        out_shape=jax.ShapeDtypeStruct((stations, 2, (block_len + 3 * bank) // 2), jnp.bfloat16),
        in_specs=[pl.BlockSpec(memory_space=pltpu.HBM)] * 3,
        out_specs=in_vmem,
        scratch_shapes=[
            *[pltpu.VMEM(given.shape, given.dtype) for given in (waveforms, moveouts, channel_mask)],
            pltpu.SemaphoreType.DMA((3,)),
        ],
    )(waveforms, moveouts, channel_mask)
    here = lax.all_to_all(packed, "sta", 0, 0, tiled=True)
    count = lax.axis_size("tm")
    after = lax.ppermute(here, "tm", [(i, i - 1) for i in range(1, count)])

    here, templates = lax.optimization_barrier((here, templates))
    fields = here[:, 1, block_len - here.shape[2] :].astype(jnp.int32)
    coarse, fine, mask = jnp.split(fields, 3, axis=1)
    first = jnp.arange(bank)[None, :] * ROW_STEP
    base = jnp.where(mask != 0, first + coarse, bank * ROW_STEP)
    places = jnp.concatenate([base, LANES - fine], axis=0).reshape(-1)
    bank_rows = jnp.pad(templates, ((0, 0), (0, depth - template_len)))

    return pl.pallas_call(
        functools.partial(
            stack_kernel, template_len=template_len, stations=stations, block_len=block_len, bank=bank
        ),
        out_shape=jax.ShapeDtypeStruct((bank, block_len), jnp.bfloat16),
        in_specs=[in_vmem] * 4,
        out_specs=pl.BlockSpec(memory_space=pl.ANY),
        scratch_shapes=[
            pltpu.SMEM((2 * stations * bank,), jnp.int32),
            pltpu.SemaphoreType.DMA,
            pltpu.VMEM((bank, block_len), jnp.bfloat16),
            pltpu.SemaphoreType.DMA((bank // PIECE,)),
            pltpu.VMEM((stations, 2 * block_len + LANES), jnp.float32),
            pltpu.VMEM((8 * stations * (2 * block_len // LANES + 1), LANES), jnp.float32),
            *[pltpu.VMEM((depth, blocks * LANES), jnp.bfloat16)] * 4,
            *[pltpu.VMEM((bank * ROW_STEP + 16, LANES), jnp.float32)] * 4,
            pltpu.VMEM((bank * block_len // LANES, LANES), jnp.float32),
        ],
        compiler_params=pltpu.CompilerParams(vmem_limit_bytes=48 * 1024 * 1024),
    )(places, here, after, bank_rows)


def solution(mesh):
    in_specs = (P("sta", "tm"), P("tpl", None), P("sta", "tpl"), P("sta", "tpl"))
    out_specs = P("tpl", "tm")
    return jax.shard_map(shards, mesh=mesh, in_specs=in_specs, out_specs=out_specs, check_vma=False)
```

time: 37.3 us -> 32.7 us (0.88)
  Pallas kernels: 14 us -> 9.46 us
    pallas_call x1, Pallas kernels: 12.7 us -> 8.06 us  [shards(): pl.pallas_call(functools.partial(stack_kernel, template_len=template_len,...]
where the time goes in v2:
time: 32.7 us; the launch traced here: 32.5 us
  starting transfers between devices  16 us (49%)
  Pallas kernels  9.46 us (29%)
  waiting for transfers between devices  6.71 us (21%)
    ppermute x1, starting transfers between devices, shards(): after = lax.ppermute(here, 'tm', [(i, i - 1) for i in range(1, count)])  11.7 us
    pallas_call x1, Pallas kernels, shards(): pl.pallas_call(functools.partial(stack_kernel, template_len=template_len,...  8.06 us
    all_to_all x1, waiting for transfers between devices, shards(): here = lax.all_to_all(packed, 'sta', 0, 0, tiled=True)  5.42 us
    all_to_all x1, starting transfers between devices, shards(): here = lax.all_to_all(packed, 'sta', 0, 0, tiled=True)  4.31 us
    pallas_call x1, Pallas kernels, shards(): pl.pallas_call(pack_kernel, out_shape=jax.ShapeDtypeStruct((stations, 2,...  1.39 us
    ppermute x1, waiting for transfers between devices, shards(): after = lax.ppermute(here, 'tm', [(i, i - 1) for i in range(1, count)])  1.29 us
  transfers between devices with their start and end apart: 2, of which 2 were waited for; matrix products, arithmetic and copies ran while one was open for 1% of the time, Pallas kernels for 0%

profile of v2, /device:TPU:40, one launch (start us, length us, event | category | flops | bytes accessed | tf_op | source)
XLA Modules:
  0.0 32.5 jit_solution(10248000522728540049)
XLA Ops:
  0.0 0.0 copy-start
  0.0 1.4 %shard_map.46 = bf16[8,2,896]{2,1,0:T(2,128)(2,1)} custom-call(bf16[1,1024]{1,0:T(2,128)(2,1)} %wave_hbm.1, s32[1,256]{1,0:T(1,128)} %moves_hbm.1, s32[1,256]{1,0:T(1,128)} %mask_hbm.1), custom_call_target="tpu_custom_call" | custom-call | tf_op jit(solution)/shard_map/pallas_call | solution.py:165
  1.4 4.3 %all-to-all-start = ((bf16[8,2,896]{2,1,0:T(2,128)(2,1)}), bf16[8,2,896]{2,1,0:T(2,128)(2,1)S(1)}, u32[]{:S(2)}, u32[]{:S(2)}) async-start(bf16[8,2,896]{2,1,0:T(2,128)(2,1)} %shard_map.46), calls=%async_computation | async-start | bytes 57344 | tf_op jit(solution)/shard_map/all_to_all | solution.py:175
  5.7 5.4 %all-to-all-done.here_ref = bf16[8,2,896]{2,1,0:T(2,128)(2,1)S(1)} async-done(((bf16[8,2,896]{2,1,0:T(2,128)(2,1)}), bf16[8,2,896]{2,1,0:T(2,128)(2,1)S(1)}, u32[]{:S(2)}, u32[]{:S(2)}) %all-to-all-start) | async-done | bytes 28704 | tf_op jit(solution)/shard_map/all_to_all | solution.py:175
  11.2 11.7 %collective-permute-start = (bf16[8,2,896]{2,1,0:T(2,128)(2,1)S(1)}, bf16[8,2,896]{2,1,0:T(2,128)(2,1)S(1)}, u32[]{:S(2)}, u32[]{:S(2)}) collective-permute-start(bf16[8,2,896]{2,1,0:T(2,128)(2,1)S(1)} %all-to-all-done.here_ref), channel_id=1, source_target_pairs={{2,0},{4,2},{6,4},{8,6},{10,8},{12,10},{14,12},{16,14},{18,16},{20... | collective-permute-start | bytes 86024 | tf_op jit(solution)/shard_map/ppermute | solution.py:177
  23.0 0.0 copy-done
  23.0 0.2 copy.5
  23.2 1.3 %collective-permute-done.next_ref = bf16[8,2,896]{2,1,0:T(2,128)(2,1)S(1)} collective-permute-done((bf16[8,2,896]{2,1,0:T(2,128)(2,1)S(1)}, bf16[8,2,896]{2,1,0:T(2,128)(2,1)S(1)}, u32[]{:S(2)}, u32[]{:S(2)}) %collective-permute-start) | collective-permute-done | bytes 28704 | tf_op jit(solution)/shard_map/ppermute | solution.py:177
  24.5 8.1 %shard_map.47 = bf16[256,1024]{1,0:T(8,128)(2,1)} custom-call(s32[4096]{0:T(1024)S(1)} %bitcast.6, bf16[8,2,896]{2,1,0:T(2,128)(2,1)S(1)} %all-to-all-done.here_ref, bf16[8,2,896]{2,1,0:T(2,128)(2,1)S(1)} %collective-permute-done.next_ref, bf16[256,304]{1,0:T(8,128)(2,1)S(1)} %pad.4.bank_ref), custom_call_target="tpu_custom_call" | custom-call | tf_op jit(solution)/shard_map/pallas_call | solution.py:187
  (7 shorter events, 0.1 us)
Async XLA Ops:
  0.0 23.0 %copy-start = (bf16[256,300]{0,1:T(8,128)(2,1)S(1)}, bf16[256,300]{0,1:T(8,128)(2,1)}, u32[]{:S(2)}) copy-start(bf16[256,300]{0,1:T(8,128)(2,1)} %param.5) | copy-start | bytes 460804
  1.4 9.7 %all-to-all-start = ((bf16[8,2,896]{2,1,0:T(2,128)(2,1)}), bf16[8,2,896]{2,1,0:T(2,128)(2,1)S(1)}, u32[]{:S(2)}, u32[]{:S(2)}) async-start(bf16[8,2,896]{2,1,0:T(2,128)(2,1)} %shard_map.46), calls=%async_computation | async-start | bytes 57344 | tf_op jit(solution)/shard_map/all_to_all | solution.py:175
  11.2 13.3 %collective-permute-start = (bf16[8,2,896]{2,1,0:T(2,128)(2,1)S(1)}, bf16[8,2,896]{2,1,0:T(2,128)(2,1)S(1)}, u32[]{:S(2)}, u32[]{:S(2)}) collective-permute-start(bf16[8,2,896]{2,1,0:T(2,128)(2,1)S(1)} %all-to-all-done.here_ref), channel_id=1, source_target_pairs={{2,0},{4,2},{6,4},{8,6},{10,8},{12,10},{14,12},{16,14},{18,16},{20... | collective-permute-start | bytes 86024 | tf_op jit(solution)/shard_map/ppermute | solution.py:177

commit v3 on v2

--- a/solution.py
+++ b/solution.py
@@ -20,15 +20,9 @@
     return x if by == 0 else pltpu.roll(x, x.shape[1] - by, 1)
 
 
-def pack_kernel(wave_hbm, moves_hbm, mask_hbm, out_ref, wave_ref, moves_ref, mask_ref, sems):
-    given = ((wave_hbm, wave_ref), (moves_hbm, moves_ref), (mask_hbm, mask_ref))
-    copies = [pltpu.make_async_copy(source, target, sems.at[i]) for i, (source, target) in enumerate(given)]
-    for copy in copies:
-        copy.start()
-    for copy in copies:
-        copy.wait()
-    moves = moves_ref[...]
-    fields = (wave_ref[...].astype(jnp.float32), moves >> 7, moves & 127, mask_ref[...])
+def pack_kernel(known_ref, after_ref, out_ref):
+    block_len = after_ref.shape[1]
+    fields = (known_ref[:, :block_len], after_ref[...], known_ref[:, block_len:])
     line = jnp.concatenate([field.astype(jnp.float32) for field in fields], axis=1)
     half = line.shape[1] // 2
     lines = jnp.concatenate([line[:, :half], line[:, half:]], axis=0).astype(jnp.bfloat16)
@@ -36,7 +30,7 @@
 
 
 def stack_kernel(
-    moves_ref, here_ref, next_ref, bank_ref, out_ref,
+    moves_ref, here_ref, bank_ref, out_ref,
     places, moves_sem, stacked, out_sem, rms_ref, rows_ref, toeplitz_a, toeplitz_b, toeplitz_c, toeplitz_d, normed_a, normed_b, normed_c, normed_d, total,
     *, template_len, stations, block_len, bank,
 ):
@@ -49,9 +43,7 @@
     samples = jnp.concatenate(
         [
             here_ref[:, 0, :].astype(jnp.float32),
-            here_ref[:, 1, : block_len - half].astype(jnp.float32),
-            next_ref[:, 0, :].astype(jnp.float32),
-            next_ref[:, 1, : block_len - half].astype(jnp.float32),
+            here_ref[:, 1, : 2 * block_len - half].astype(jnp.float32),
             jnp.zeros((stations, LANES), jnp.float32),
         ],
         axis=1,
@@ -162,22 +154,19 @@
     blocks = -(-(block_len + MOVE) // (2 * LANES)) * 2
     in_vmem = pl.BlockSpec(memory_space=pltpu.VMEM)
 
+    count = lax.axis_size("tm")
+    after = lax.ppermute(waveforms, "tm", [(i, i - 1) for i in range(1, count)])
+    fields = (waveforms, moveouts >> 7, moveouts & 127, channel_mask)
+    known = jnp.concatenate([field.astype(jnp.bfloat16) for field in fields], axis=1)
     packed = pl.pallas_call(
         pack_kernel,
-        out_shape=jax.ShapeDtypeStruct((stations, 2, (block_len + 3 * bank) // 2), jnp.bfloat16),
-        in_specs=[pl.BlockSpec(memory_space=pltpu.HBM)] * 3,
+        out_shape=jax.ShapeDtypeStruct((stations, 2, (2 * block_len + 3 * bank) // 2), jnp.bfloat16),
+        in_specs=[in_vmem] * 2,
         out_specs=in_vmem,
-        scratch_shapes=[
-            *[pltpu.VMEM(given.shape, given.dtype) for given in (waveforms, moveouts, channel_mask)],
-            pltpu.SemaphoreType.DMA((3,)),
-        ],
-    )(waveforms, moveouts, channel_mask)
+        compiler_params=pltpu.CompilerParams(vmem_limit_bytes=1024 * 1024),
+    )(known, after)
     here = lax.all_to_all(packed, "sta", 0, 0, tiled=True)
-    count = lax.axis_size("tm")
-    after = lax.ppermute(here, "tm", [(i, i - 1) for i in range(1, count)])
-
-    here, templates = lax.optimization_barrier((here, templates))
-    fields = here[:, 1, block_len - here.shape[2] :].astype(jnp.int32)
+    fields = here[:, 1, 2 * block_len - here.shape[2] :].astype(jnp.int32)
     coarse, fine, mask = jnp.split(fields, 3, axis=1)
     first = jnp.arange(bank)[None, :] * ROW_STEP
     base = jnp.where(mask != 0, first + coarse, bank * ROW_STEP)
@@ -189,7 +178,7 @@
             stack_kernel, template_len=template_len, stations=stations, block_len=block_len, bank=bank
         ),
         out_shape=jax.ShapeDtypeStruct((bank, block_len), jnp.bfloat16),
-        in_specs=[in_vmem] * 4,
+        in_specs=[in_vmem] * 3,
         out_specs=pl.BlockSpec(memory_space=pl.ANY),
         scratch_shapes=[
             pltpu.SMEM((2 * stations * bank,), jnp.int32),
@@ -203,7 +192,7 @@
             pltpu.VMEM((bank * block_len // LANES, LANES), jnp.float32),
         ],
         compiler_params=pltpu.CompilerParams(vmem_limit_bytes=48 * 1024 * 1024),
-    )(places, here, after, bank_rows)
+    )(places, here, bank_rows)
 
 
 def solution(mesh):

time: 32.7 us -> 32.2 us (0.985)
  the two profiles are of different devices: /device:TPU:40 before, /device:TPU:48 now
where the time goes in v3:
time: 32.2 us; the launch traced here: 32 us
  starting transfers between devices  16.1 us (50%)
  Pallas kernels  8.68 us (27%)
  waiting for transfers between devices  5.43 us (17%)
  other arithmetic  1.44 us (4%)
    ppermute x1, starting transfers between devices, shards(): after = lax.ppermute(waveforms, 'tm', [(i, i - 1) for i in range(1, count)])  11.8 us
    pallas_call x1, Pallas kernels, shards(): pl.pallas_call(functools.partial(stack_kernel, template_len=template_len,...  8.04 us
    all_to_all x1, waiting for transfers between devices, shards(): here = lax.all_to_all(packed, 'sta', 0, 0, tiled=True)  5.29 us
    all_to_all x1, starting transfers between devices, shards(): here = lax.all_to_all(packed, 'sta', 0, 0, tiled=True)  4.3 us
    convert_element_type x2, other arithmetic, shards(): field.astype(jnp.bfloat16)  1.37 us
  transfers between devices with their start and end apart: 2, of which 2 were waited for; matrix products, arithmetic and copies ran while one was open for 5% of the time, Pallas kernels for 0%

profile of v3, /device:TPU:48, one launch (start us, length us, event | category | flops | bytes accessed | tf_op | source)
XLA Modules:
  0.0 32.0 jit_solution(8286563575189668915)
XLA Ops:
  0.0 0.0 copy-start.1
  0.0 0.0 copy-start
  0.0 11.8 %collective-permute-start = (bf16[1,1024]{1,0:T(2,128)(2,1)}, bf16[1,1024]{1,0:T(2,128)(2,1)S(1)}, u32[]{:S(2)}, u32[]{:S(2)}) collective-permute-start(bf16[1,1024]{1,0:T(2,128)(2,1)} %param.4), channel_id=1, source_target_pairs={{2,0},{4,2},{6,4},{8,6},{10,8},{12,10},{14,12},{16,14},{18,16},{20... | collective-permute-start | bytes 6152 | tf_op jit(solution)/shard_map/ppermute | solution.py:158
  11.9 0.7 %convert_element_type.19 = bf16[1,256]{1,0:T(2,128)(2,1)S(1)} convert(s32[1,256]{1,0:T(1,128)} %param.7) | non-fusion elementwise | flops 256 | bytes 1536 | tf_op jit(solution)/shard_map/convert_element_type | solution.py:160
  12.5 0.7 %shift-right-arithmetic_convert_fusion = (bf16[1,256]{1,0:T(2,128)(2,1)S(1)}, bf16[1,256]{1,0:T(2,128)(2,1)S(1)}) fusion(s32[1,256]{1,0:T(1,128)} %param.6), kind=kLoop, calls=%fused_computation.10 | loop fusion | flops 1024 | bytes 2048 | tf_op jit(solution)/shard_map/convert_element_type | solution.py:160
  13.2 0.0 copy-done.1
  13.2 0.1 collective-permute-done.after_ref
  13.4 0.6 %shard_map.46 = bf16[8,2,1408]{2,1,0:T(2,128)(2,1)} custom-call(bf16[1,1792]{1,0:T(2,128)(2,1)S(1)} %pad_maximum_fusion.known_ref, bf16[1,1024]{1,0:T(2,128)(2,1)S(1)} %collective-permute-done.after_ref), custom_call_target="tpu_custom_call" | custom-call | tf_op jit(solution)/shard_map/pallas_call | solution.py:161
  14.0 4.3 %all-to-all-start = ((bf16[8,2,1408]{2,1,0:T(2,128)(2,1)}), bf16[8,2,1408]{2,1,0:T(2,128)(2,1)S(1)}, u32[]{:S(2)}, u32[]{:S(2)}) async-start(bf16[8,2,1408]{2,1,0:T(2,128)(2,1)} %shard_map.46), calls=%async_computation | async-start | bytes 90112 | tf_op jit(solution)/shard_map/all_to_all | solution.py:168
  18.3 0.0 copy-done
  18.3 0.2 copy.5
  18.5 5.3 %all-to-all-done.here_ref = bf16[8,2,1408]{2,1,0:T(2,128)(2,1)S(1)} async-done(((bf16[8,2,1408]{2,1,0:T(2,128)(2,1)}), bf16[8,2,1408]{2,1,0:T(2,128)(2,1)S(1)}, u32[]{:S(2)}, u32[]{:S(2)}) %all-to-all-start) | async-done | bytes 45088 | tf_op jit(solution)/shard_map/all_to_all | solution.py:168
  23.9 8.0 %shard_map.47 = bf16[256,1024]{1,0:T(8,128)(2,1)} custom-call(s32[4096]{0:T(1024)S(1)} %bitcast.6, bf16[8,2,1408]{2,1,0:T(2,128)(2,1)S(1)} %all-to-all-done.here_ref, bf16[256,304]{1,0:T(8,128)(2,1)S(1)} %pad.4.bank_ref), custom_call_target="tpu_custom_call" | custom-call | tf_op jit(solution)/shard_map/pallas_call | solution.py:176
  (8 shorter events, 0.1 us)
Async XLA Ops:
  0.0 13.2 %copy-start.1 = (bf16[1,1024]{1,0:T(2,128)(2,1)S(1)}, bf16[1,1024]{1,0:T(2,128)(2,1)}, u32[]{:S(2)}) copy-start(bf16[1,1024]{1,0:T(2,128)(2,1)} %param.4) | copy-start | bytes 6148
  0.0 18.3 %copy-start = (bf16[256,300]{0,1:T(8,128)(2,1)S(1)}, bf16[256,300]{0,1:T(8,128)(2,1)}, u32[]{:S(2)}) copy-start(bf16[256,300]{0,1:T(8,128)(2,1)} %param.5) | copy-start | bytes 460804
  0.0 13.4 %collective-permute-start = (bf16[1,1024]{1,0:T(2,128)(2,1)}, bf16[1,1024]{1,0:T(2,128)(2,1)S(1)}, u32[]{:S(2)}, u32[]{:S(2)}) collective-permute-start(bf16[1,1024]{1,0:T(2,128)(2,1)} %param.4), channel_id=1, source_target_pairs={{2,0},{4,2},{6,4},{8,6},{10,8},{12,10},{14,12},{16,14},{18,16},{20... | collective-permute-start | bytes 6152 | tf_op jit(solution)/shard_map/ppermute | solution.py:158
  14.0 9.8 %all-to-all-start = ((bf16[8,2,1408]{2,1,0:T(2,128)(2,1)}), bf16[8,2,1408]{2,1,0:T(2,128)(2,1)S(1)}, u32[]{:S(2)}, u32[]{:S(2)}) async-start(bf16[8,2,1408]{2,1,0:T(2,128)(2,1)} %shard_map.46), calls=%async_computation | async-start | bytes 90112 | tf_op jit(solution)/shard_map/all_to_all | solution.py:168

commit v4 on v3

--- a/solution.py
+++ b/solution.py
@@ -12,7 +12,6 @@
 EPSILON = 1e-05
 LANES = 128
 ROW_STEP = 17
-WIDE = 14
 PIECE = 64
 
 
@@ -83,15 +82,17 @@
             if row < depth:
                 toeplitz[row : row + 16, :] = pair[:, part * LANES : (part + blocks) * LANES]
 
-    def correlate(s, toeplitz, normed, first, last):
-        span = slice(first * LANES, last * LANES)
-        correlated = jnp.dot(bank_ref[...], toeplitz[:, span], preferred_element_type=jnp.float32)
-        scaled = correlated * rms_ref[s : s + 1, span]
-        for k in range(0, bank, 8):
-            for block in range(first, last):
-                row = k * ROW_STEP + block
-                column = (block - first) * LANES
-                normed[pl.ds(row, 8, stride=ROW_STEP), :] = scaled[k : k + 8, column : column + LANES]
+    def correlate(members, toeplitz, normed):
+        taps = jnp.concatenate([one[...] for one in toeplitz[: len(members)]], axis=1)
+        rms = jnp.concatenate([rms_ref[s : s + 1, : blocks * LANES] for s in members], axis=1)
+        scaled = jnp.dot(bank_ref[...], taps, preferred_element_type=jnp.float32) * rms
+        for one in range(len(members)):
+            for k in range(0, bank, 8):
+                for block in range(blocks):
+                    column = (one * blocks + block) * LANES
+                    normed[one][pl.ds(k * ROW_STEP + block, 8, stride=ROW_STEP), :] = scaled[
+                        k : k + 8, column : column + LANES
+                    ]
 
     def add_moved(members, buffers, templates):
         for k in templates:
@@ -109,20 +110,17 @@
 
     toeplitz = ((toeplitz_a, toeplitz_b), (toeplitz_c, toeplitz_d))
     normed = ((normed_a, normed_b), (normed_c, normed_d))
-    members = [(s, s + 1) for s in range(0, stations - 2, 2)] + [(stations - 2,), (stations - 1,)]
-    spans = [(first, min(first + WIDE, blocks)) for first in range(0, blocks, WIDE)]
+    members = [(s, s + 1) for s in range(0, stations, 2)]
     groups = LANES // 16
 
     def stage(p):
-        jobs = [(one, span) for span in spans for one in range(len(members[p]))]
-        for j, (one, span) in enumerate(jobs):
-            share = lambda amount: range(amount * j // len(jobs), amount * (j + 1) // len(jobs))
-            correlate(members[p][one], toeplitz[p % 2][one], normed[p % 2][one], *span)
-            if p + 1 < len(members):
-                for step in share(len(members[p + 1]) * groups):
-                    lay_out(members[p + 1][step // groups], step % groups, toeplitz[(p + 1) % 2][step // groups])
-            if p > 0:
-                add_moved(members[p - 1], normed[(p - 1) % 2], share(bank))
+        correlate(members[p], toeplitz[p % 2], normed[p % 2])
+        if p + 1 < len(members):
+            for one, s in enumerate(members[p + 1]):
+                for group in range(groups):
+                    lay_out(s, group, toeplitz[(p + 1) % 2][one])
+        if p > 0:
+            add_moved(members[p - 1], normed[(p - 1) % 2], range(bank))
 
     for one in range(2):
         for group in range(groups):

time: 32.2 us -> 31.9 us (level)
  the two profiles are of different devices: /device:TPU:48 before, /device:TPU:40 now
where the time goes in v4:
time: 31.9 us; the launch traced here: 31.7 us
  starting transfers between devices  16.1 us (50%)
  Pallas kernels  8.39 us (26%)
  waiting for transfers between devices  5.43 us (17%)
  other arithmetic  1.44 us (5%)
    ppermute x1, starting transfers between devices, shards(): after = lax.ppermute(waveforms, 'tm', [(i, i - 1) for i in range(1, count)])  11.8 us
    pallas_call x1, Pallas kernels, shards(): pl.pallas_call(functools.partial(stack_kernel, template_len=template_len,...  7.75 us
    all_to_all x1, waiting for transfers between devices, shards(): here = lax.all_to_all(packed, 'sta', 0, 0, tiled=True)  5.29 us
    all_to_all x1, starting transfers between devices, shards(): here = lax.all_to_all(packed, 'sta', 0, 0, tiled=True)  4.3 us
    convert_element_type x2, other arithmetic, shards(): field.astype(jnp.bfloat16)  1.37 us
  transfers between devices with their start and end apart: 2, of which 2 were waited for; matrix products, arithmetic and copies ran while one was open for 5% of the time, Pallas kernels for 0%

profile of v4, /device:TPU:40, one launch (start us, length us, event | category | flops | bytes accessed | tf_op | source)
XLA Modules:
  0.0 31.7 jit_solution(13824003250366150789)
XLA Ops:
  0.0 0.0 copy-start.1
  0.0 0.0 copy-start
  0.0 11.8 %collective-permute-start = (bf16[1,1024]{1,0:T(2,128)(2,1)}, bf16[1,1024]{1,0:T(2,128)(2,1)S(1)}, u32[]{:S(2)}, u32[]{:S(2)}) collective-permute-start(bf16[1,1024]{1,0:T(2,128)(2,1)} %param.4), channel_id=1, source_target_pairs={{2,0},{4,2},{6,4},{8,6},{10,8},{12,10},{14,12},{16,14},{18,16},{20... | collective-permute-start | bytes 6152 | tf_op jit(solution)/shard_map/ppermute | solution.py:156
  11.9 0.7 %convert_element_type.19 = bf16[1,256]{1,0:T(2,128)(2,1)S(1)} convert(s32[1,256]{1,0:T(1,128)} %param.7) | non-fusion elementwise | flops 256 | bytes 1536 | tf_op jit(solution)/shard_map/convert_element_type | solution.py:158
  12.5 0.7 %shift-right-arithmetic_convert_fusion = (bf16[1,256]{1,0:T(2,128)(2,1)S(1)}, bf16[1,256]{1,0:T(2,128)(2,1)S(1)}) fusion(s32[1,256]{1,0:T(1,128)} %param.6), kind=kLoop, calls=%fused_computation.10 | loop fusion | flops 1024 | bytes 2048 | tf_op jit(solution)/shard_map/convert_element_type | solution.py:158
  13.2 0.0 copy-done.1
  13.2 0.1 collective-permute-done.after_ref
  13.4 0.6 %shard_map.46 = bf16[8,2,1408]{2,1,0:T(2,128)(2,1)} custom-call(bf16[1,1792]{1,0:T(2,128)(2,1)S(1)} %pad_maximum_fusion.known_ref, bf16[1,1024]{1,0:T(2,128)(2,1)S(1)} %collective-permute-done.after_ref), custom_call_target="tpu_custom_call" | custom-call | tf_op jit(solution)/shard_map/pallas_call | solution.py:159
  14.0 4.3 %all-to-all-start = ((bf16[8,2,1408]{2,1,0:T(2,128)(2,1)}), bf16[8,2,1408]{2,1,0:T(2,128)(2,1)S(1)}, u32[]{:S(2)}, u32[]{:S(2)}) async-start(bf16[8,2,1408]{2,1,0:T(2,128)(2,1)} %shard_map.46), calls=%async_computation | async-start | bytes 90112 | tf_op jit(solution)/shard_map/all_to_all | solution.py:166
  18.3 0.0 copy-done
  18.3 0.2 copy.5
  18.5 5.3 %all-to-all-done.here_ref = bf16[8,2,1408]{2,1,0:T(2,128)(2,1)S(1)} async-done(((bf16[8,2,1408]{2,1,0:T(2,128)(2,1)}), bf16[8,2,1408]{2,1,0:T(2,128)(2,1)S(1)}, u32[]{:S(2)}, u32[]{:S(2)}) %all-to-all-start) | async-done | bytes 45088 | tf_op jit(solution)/shard_map/all_to_all | solution.py:166
  23.9 7.7 %shard_map.47 = bf16[256,1024]{1,0:T(8,128)(2,1)} custom-call(s32[4096]{0:T(1024)S(1)} %bitcast.6, bf16[8,2,1408]{2,1,0:T(2,128)(2,1)S(1)} %all-to-all-done.here_ref, bf16[256,304]{1,0:T(8,128)(2,1)S(1)} %pad.4.bank_ref), custom_call_target="tpu_custom_call" | custom-call | tf_op jit(solution)/shard_map/pallas_call | solution.py:174
  (8 shorter events, 0.1 us)
Async XLA Ops:
  0.0 13.2 %copy-start.1 = (bf16[1,1024]{1,0:T(2,128)(2,1)S(1)}, bf16[1,1024]{1,0:T(2,128)(2,1)}, u32[]{:S(2)}) copy-start(bf16[1,1024]{1,0:T(2,128)(2,1)} %param.4) | copy-start | bytes 6148
  0.0 18.3 %copy-start = (bf16[256,300]{0,1:T(8,128)(2,1)S(1)}, bf16[256,300]{0,1:T(8,128)(2,1)}, u32[]{:S(2)}) copy-start(bf16[256,300]{0,1:T(8,128)(2,1)} %param.5) | copy-start | bytes 460804
  0.0 13.4 %collective-permute-start = (bf16[1,1024]{1,0:T(2,128)(2,1)}, bf16[1,1024]{1,0:T(2,128)(2,1)S(1)}, u32[]{:S(2)}, u32[]{:S(2)}) collective-permute-start(bf16[1,1024]{1,0:T(2,128)(2,1)} %param.4), channel_id=1, source_target_pairs={{2,0},{4,2},{6,4},{8,6},{10,8},{12,10},{14,12},{16,14},{18,16},{20... | collective-permute-start | bytes 6152 | tf_op jit(solution)/shard_map/ppermute | solution.py:156
  14.0 9.8 %all-to-all-start = ((bf16[8,2,1408]{2,1,0:T(2,128)(2,1)}), bf16[8,2,1408]{2,1,0:T(2,128)(2,1)S(1)}, u32[]{:S(2)}, u32[]{:S(2)}) async-start(bf16[8,2,1408]{2,1,0:T(2,128)(2,1)} %shard_map.46), calls=%async_computation | async-start | bytes 90112 | tf_op jit(solution)/shard_map/all_to_all | solution.py:166
